TPU v7x, 128 devices: a whole 4x4x4 slice. The times are simulated.
128 devices in a mesh: in: 8 (over z, core), out: 16 (over x, y).
Axes of the slice: x: 4, y: 4, z: 4, core: 2. Of those that a mesh axis runs over, the one named last changes fastest.
Arguments:
- activations: bfloat16 [1024, 5120], P('out', 'in'), may hold values from -6 to 6
- act_basis: bfloat16 [5120, 5120], P(None, 'in'), may hold values from -0.078125 to 0.078125
- gradients: bfloat16 [1024, 20480], P('out', 'in'), may hold values from -0.59765625 to 0.59765625
- grad_basis: bfloat16 [20480, 20480], P('in', 'out'), may hold values from -0.0390625 to 0.0390625
- lengths: int32 [8], replicated, may hold values from 1 to 128, 768 in all
- sample_weights: int32 [8], replicated, may hold values from 1 to 4
Outputs:
- eigenvalues: float32 [20480, 5120], P('out', 'in')
Inputs may be any that keep to these rules, and one draw needn't show every extreme that they name: Some sequence is full, every sequence has at least one valid token, and the lengths sum to 768.
All inputs are finite; a program needn't handle non-finite values.
Results may differ from a plain program's by a relative error of at most 0.0031.
Values may be sent and summed in bfloat16 or wider, within the bound.
A program may use at most 128 MiB of HBM per device.

v0:
```python
import jax
import jax.numpy as jnp
from jax import lax
from jax.sharding import PartitionSpec as P


def local(activations, act_basis, gradients, grad_basis, lengths, sample_weights):
    width_in = act_basis.shape[1]
    all_slots = lax.all_gather(activations, "out", axis=0, tiled=True)
    rot_act = jnp.dot(
        lax.all_gather(all_slots, "in", axis=1, tiled=True),
        act_basis,
        preferred_element_type=jnp.float32,
    ).astype(jnp.bfloat16)
    seq_count = lengths.shape[0]
    slot_count = rot_act.shape[0] // seq_count
    positions = jnp.arange(slot_count, dtype=jnp.int32)
    valid_flags = positions[None, :] < lengths[:, None]
    valid = valid_flags.astype(jnp.bfloat16)
    partial_rot = jnp.dot(
        lax.all_gather(gradients, "out", axis=0, tiled=True),
        grad_basis,
        preferred_element_type=jnp.float32,
    )
    rot_rows = lax.psum(partial_rot, "in").astype(jnp.bfloat16)
    act_seq = rot_act.reshape(seq_count, slot_count, width_in)
    grad_seq = rot_rows.reshape(seq_count, slot_count, rot_rows.shape[1]) * valid[:, :, None]
    weights = sample_weights.astype(jnp.float32)

    def accumulate(total, item):
        grad_one, act_one, weight = item
        block = lax.dot_general(
            grad_one, act_one, (((0,), (0,)), ((), ())), preferred_element_type=jnp.float32
        )
        return (total + weight * block * block, None)

    start_total = jnp.zeros((rot_rows.shape[1], width_in), jnp.float32)
    total, unused = lax.scan(accumulate, start_total, (grad_seq, act_seq, weights))
    return total / jnp.sum(weights)


def solution(mesh):
    in_specs = (P("out", "in"), P(None, "in"), P("out", "in"), P("in", "out"), P(), P())
    out_specs = P("out", "in")
    return jax.shard_map(local, mesh=mesh, in_specs=in_specs, out_specs=out_specs, check_vma=False)
```

profile of v0, /device:TPU:1, one launch (start us, length us, event | category | flops | bytes accessed | tf_op | source)
XLA Modules:
  0.0 280.9 jit_solution(611817423196145019)
XLA Ops:
  6.5 0.0 all-gather.6.cloned.1.call-start
  6.5 0.7 all-gather.6.cloned.1.call-update
  7.3 0.0 all-gather.4.cloned.1.call-start
  7.3 0.7 all-gather.4.cloned.1.call-update
  8.0 0.0 all-gather.8.cloned.1.call-start
  8.1 47.1 %all-gather.6.cloned.1.call-done = bf16[1024,640]{1,0:T(8,128)(2,1)} async-done(((bf16[64,640]{1,0:T(8,128)(2,1)}), bf16[1024,640]{1,0:T(8,128)(2,1)}) %all-gather.6.cloned.1.call-update) | async-done | bytes 1310736 | tf_op jit(solution)/shard_map/all_gather | solution.py:9
  55.2 0.0 all-gather.8.cloned.1.call-update
  55.2 0.7 convert_element_type.16
  55.9 1.3 convert_reduce_fusion
  57.2 0.7 fusion.6
  57.9 56.0 %all-gather.4.cloned.1.call-done = bf16[1024,2560]{1,0:T(8,128)(2,1)} async-done(((bf16[64,2560]{1,0:T(8,128)(2,1)}), bf16[1024,2560]{1,0:T(8,128)(2,1)}) %all-gather.4.cloned.1.call-update) | async-done | bytes 5242896 | tf_op jit(solution)/shard_map/all_gather | solution.py:21
  113.9 12.2 %fusion.7 = f32[1024,1280]{1,0:T(8,128)} fusion(bf16[1024,2560]{1,0:T(8,128)(2,1)} %all-gather.4.cloned.1.call-done, bf16[2560,1280]{1,0:T(8,128)(2,1)} %param.11), kind=kOutput, calls=%fused_computation.13 | convolution fusion | flops 6710886400 | bytes 17039360 | tf_op jit(solution)/shard_map/dot_general | solution.py:20
  126.1 100.5 %all-reduce.1 = bf16[1024,1280]{1,0:T(8,128)(2,1)} all-reduce(f32[1024,1280]{1,0:T(8,128)} %fusion.7), channel_id=1, replica_groups=mesh['in'=8,'out'=16] {'in'}, use_global_device_ids=true, to_apply=%region_0.0 | all-reduce | flops 1310720 | bytes 7864320 | tf_op jit(solution)/shard_map/psum | solution.py:25
  226.6 3.5 %broadcast_multiply_fusion = bf16[8,128,1280]{2,1,0:T(8,128)(2,1)} fusion(bf16[8,128,1280]{2,1,0:T(8,128)(2,1)} %bitcast.19, bf16[8,128]{1,0:T(8,128)(2,1)S(1)} %fusion.6), kind=kLoop, calls=%fused_computation.9 | loop fusion | flops 1310720 | bytes 5244928 | tf_op jit(solution)/shard_map/mul | solution.py:27
  230.1 0.0 all-gather.8.cloned.1.call-done
  230.1 13.7 %convolution_convert_fusion = bf16[1024,640]{1,0:T(8,128)(2,1)} fusion(bf16[1024,5120]{1,0:T(8,128)(2,1)} %all-gather.8.cloned.1.call-done, bf16[5120,640]{1,0:T(8,128)(2,1)} %param.9), kind=kOutput, calls=%fused_computation.8 | convolution fusion | flops 6711541760 | bytes 18350080 | tf_op jit(solution)/shard_map/dot_general | solution.py:10
  243.8 27.9 %while.11 = (s32[]{:T(128)}, f32[1280,640]{1,0:T(8,128)S(1)}, f32[8]{0:T(128)S(1)}, bf16[8,128,1280]{2,1,0:T(8,128)(2,1)}, bf16[8,128,640]{2,1,0:T(8,128)(2,1)}, /*index=5*/s32[]{:T(128)}, s32[]{:T(128)}) while((s32[]{:T(128)}, f32[1280,640]{1,0:T(8,128)S(1)}, f32[8]{0:T(128)S(1)}, bf16[8,128,1280]{2,1,0:T(8,128)(2,1)}, ...), condition=%wide.region_2.3_spmd.clone, body=%wide.region_1.2_spmd.clone.sunk | while | flops 212992000 | bytes 7047274 | solution.py:38
  243.8 0.6 dynamic_slice.28
  244.4 2.9 %fusion.17 = f32[1280,640]{1,0:T(8,128)S(1)} fusion(f32[1280,640]{1,0:T(8,128)S(1)} %get-tuple-element.100, f32[]{:T(128)} %bitcast.18, pred[]{:T(512)S(6)} %compare.3, bf16[8,128,1280]{2,1,0:T(8,128)(2,1)} %get-tuple-element.109, s32[]{:T(128)S(6)} %copy.10, bf16[8,128,640]{2,1,0:T(8,128)(2,1)} %get-tuple-element.110), kind=kOutput, calls=%fused_computation.1.clone.1 | convolution fusion | flops 212992000 | bytes 7047168 | tf_op jit(solution)/shard_map/while/body/eval_jaxpr/dot_general | solution.py:32
  247.3 0.6 dynamic_slice.28
  247.9 2.9 %fusion.17 = f32[1280,640]{1,0:T(8,128)S(1)} fusion(f32[1280,640]{1,0:T(8,128)S(1)} %get-tuple-element.100, f32[]{:T(128)} %bitcast.18, pred[]{:T(512)S(6)} %compare.3, bf16[8,128,1280]{2,1,0:T(8,128)(2,1)} %get-tuple-element.109, s32[]{:T(128)S(6)} %copy.10, bf16[8,128,640]{2,1,0:T(8,128)(2,1)} %get-tuple-element.110), kind=kOutput, calls=%fused_computation.1.clone.1 | convolution fusion | flops 212992000 | bytes 7047168 | tf_op jit(solution)/shard_map/while/body/eval_jaxpr/dot_general | solution.py:32
  250.8 0.6 dynamic_slice.28
  251.4 2.9 %fusion.17 = f32[1280,640]{1,0:T(8,128)S(1)} fusion(f32[1280,640]{1,0:T(8,128)S(1)} %get-tuple-element.100, f32[]{:T(128)} %bitcast.18, pred[]{:T(512)S(6)} %compare.3, bf16[8,128,1280]{2,1,0:T(8,128)(2,1)} %get-tuple-element.109, s32[]{:T(128)S(6)} %copy.10, bf16[8,128,640]{2,1,0:T(8,128)(2,1)} %get-tuple-element.110), kind=kOutput, calls=%fused_computation.1.clone.1 | convolution fusion | flops 212992000 | bytes 7047168 | tf_op jit(solution)/shard_map/while/body/eval_jaxpr/dot_general | solution.py:32
  254.3 0.6 dynamic_slice.28
  254.9 2.9 %fusion.17 = f32[1280,640]{1,0:T(8,128)S(1)} fusion(f32[1280,640]{1,0:T(8,128)S(1)} %get-tuple-element.100, f32[]{:T(128)} %bitcast.18, pred[]{:T(512)S(6)} %compare.3, bf16[8,128,1280]{2,1,0:T(8,128)(2,1)} %get-tuple-element.109, s32[]{:T(128)S(6)} %copy.10, bf16[8,128,640]{2,1,0:T(8,128)(2,1)} %get-tuple-element.110), kind=kOutput, calls=%fused_computation.1.clone.1 | convolution fusion | flops 212992000 | bytes 7047168 | tf_op jit(solution)/shard_map/while/body/eval_jaxpr/dot_general | solution.py:32
  257.8 0.6 dynamic_slice.28
  258.4 2.9 %fusion.17 = f32[1280,640]{1,0:T(8,128)S(1)} fusion(f32[1280,640]{1,0:T(8,128)S(1)} %get-tuple-element.100, f32[]{:T(128)} %bitcast.18, pred[]{:T(512)S(6)} %compare.3, bf16[8,128,1280]{2,1,0:T(8,128)(2,1)} %get-tuple-element.109, s32[]{:T(128)S(6)} %copy.10, bf16[8,128,640]{2,1,0:T(8,128)(2,1)} %get-tuple-element.110), kind=kOutput, calls=%fused_computation.1.clone.1 | convolution fusion | flops 212992000 | bytes 7047168 | tf_op jit(solution)/shard_map/while/body/eval_jaxpr/dot_general | solution.py:32
  261.3 0.6 dynamic_slice.28
  261.9 2.9 %fusion.17 = f32[1280,640]{1,0:T(8,128)S(1)} fusion(f32[1280,640]{1,0:T(8,128)S(1)} %get-tuple-element.100, f32[]{:T(128)} %bitcast.18, pred[]{:T(512)S(6)} %compare.3, bf16[8,128,1280]{2,1,0:T(8,128)(2,1)} %get-tuple-element.109, s32[]{:T(128)S(6)} %copy.10, bf16[8,128,640]{2,1,0:T(8,128)(2,1)} %get-tuple-element.110), kind=kOutput, calls=%fused_computation.1.clone.1 | convolution fusion | flops 212992000 | bytes 7047168 | tf_op jit(solution)/shard_map/while/body/eval_jaxpr/dot_general | solution.py:32
  264.8 0.6 dynamic_slice.28
  265.4 2.9 %fusion.17 = f32[1280,640]{1,0:T(8,128)S(1)} fusion(f32[1280,640]{1,0:T(8,128)S(1)} %get-tuple-element.100, f32[]{:T(128)} %bitcast.18, pred[]{:T(512)S(6)} %compare.3, bf16[8,128,1280]{2,1,0:T(8,128)(2,1)} %get-tuple-element.109, s32[]{:T(128)S(6)} %copy.10, bf16[8,128,640]{2,1,0:T(8,128)(2,1)} %get-tuple-element.110), kind=kOutput, calls=%fused_computation.1.clone.1 | convolution fusion | flops 212992000 | bytes 7047168 | tf_op jit(solution)/shard_map/while/body/eval_jaxpr/dot_general | solution.py:32
  268.3 0.6 dynamic_slice.28
  268.9 2.9 %fusion.17 = f32[1280,640]{1,0:T(8,128)S(1)} fusion(f32[1280,640]{1,0:T(8,128)S(1)} %get-tuple-element.100, f32[]{:T(128)} %bitcast.18, pred[]{:T(512)S(6)} %compare.3, bf16[8,128,1280]{2,1,0:T(8,128)(2,1)} %get-tuple-element.109, s32[]{:T(128)S(6)} %copy.10, bf16[8,128,640]{2,1,0:T(8,128)(2,1)} %get-tuple-element.110), kind=kOutput, calls=%fused_computation.1.clone.1 | convolution fusion | flops 212992000 | bytes 7047168 | tf_op jit(solution)/shard_map/while/body/eval_jaxpr/dot_general | solution.py:32
  271.7 2.6 broadcast_divide_fusion
  (1 shorter events, 0.0 us)
Async XLA Ops:
  6.5 48.6 %all-gather.6.cloned.1.call-start = ((), (), s32[]{:S(2)}) async-start(), calls=%async_computation.1 | async-start | bytes 1392640 | tf_op jit(solution)/shard_map/all_gather | solution.py:9
  7.3 106.6 %all-gather.4.cloned.1.call-start = ((), (), s32[]{:S(2)}) async-start(), calls=%async_computation | async-start | bytes 5570560 | tf_op jit(solution)/shard_map/all_gather | solution.py:21
  8.0 222.1 %all-gather.8.cloned.1.call-start = ((), (), s32[]{:S(2)}) async-start(), calls=%async_computation.2 | async-start | bytes 11796480 | tf_op jit(solution)/shard_map/all_gather | solution.py:11
Sparse Core Ops, SparseCore 0:
  9.5 45.5 all-gather.5
  57.4 56.4 all-gather.3
  115.6 78.0 all-gather.7
where the time goes:
time: 284 us; the launch traced here: 281 us
  waiting for transfers between devices  105 us (37%)
  blocking collectives  101 us (36%)
  matrix products  48.9 us (17%)
  between operations  13.1 us (5%)
  other arithmetic  8.8 us (3%)
  local copies, waits for them, and re-layouts  4.76 us (2%)
    psum x1, blocking collectives, local(): rot_rows = lax.psum(partial_rot, 'in').astype(jnp.bfloat16)  101 us
    all_gather x1, waiting for transfers between devices, local(): lax.all_gather(gradients, 'out', axis=0, tiled=True)  56 us
    all_gather x1, waiting for transfers between devices, local(): all_slots = lax.all_gather(activations, 'out', axis=0, tiled=True)  47.1 us
    dot_general x8, matrix products, accumulate(): lax.dot_general(grad_one, act_one, (((0,), (0,)), ((), ())), preferred_el...  23 us
    dot_general x1, matrix products, local(): jnp.dot(lax.all_gather(all_slots, 'in', axis=1, tiled=True), act_basis, p...  13.7 us
    dot_general x1, matrix products, local(): jnp.dot(lax.all_gather(gradients, 'out', axis=0, tiled=True), grad_basis,...  12.2 us
  transfers between devices with their start and end apart: 3, of which 2 were waited for; matrix products, arithmetic and copies ran while one was open for 7% of the time, Pallas kernels for 0%

commit v1 on v0

v1 whole, which is shorter than its diff:
```python
import functools

import jax
import jax.numpy as jnp
from jax import lax
from jax.experimental import pallas as pl
from jax.experimental.pallas import tpu as pltpu
from jax.sharding import PartitionSpec as P

MESH = pl.DeviceIdType.MESH
HALF = 32
STAGES = ("own", "1", "2", "3a", "3b", "4b", "5b", "6", "7a", "7b", "8")
BRINGS = {
    "own": [(0, 0)],
    "1": [(1, 0), (-1, 0)],
    "2": [(0, 1), (0, -1)],
    "3a": [(2, 0)],
    "3b": [(1, 1), (1, -1)],
    "4b": [(-1, 1), (-1, -1)],
    "5b": [(0, 2)],
    "6": [(2, 1), (2, -1)],
    "7a": [(1, 2)],
    "7b": [(-1, 2)],
    "8": [(2, 2)],
}
SLOTS = [(lane, a, b) for stage in STAGES for lane in (0, 1) for a, b in BRINGS[stage]]
OFFSET = {slot: HALF * at for at, slot in enumerate(SLOTS)}
GROUPS = [(0, 192), (192, 128), (320, 192), (512, 192), (704, 128), (832, 128), (960, 64)]


def moves(stage):
    found = []
    for lane in (0, 1):
        for sign in (1, -1):
            part = 1 if sign == 1 else 2
            one = {
                "1": ((0, 0), (-sign, 0), 0, 0),
                "2": ((0, 0), (0, -sign), 1, 0),
                "3a": ((-sign, 0), (2, 0), 0, part),
                "3b": ((1, 0), (1, -sign), 1, 0),
                "4b": ((-1, 0), (-1, -sign), 1, 0),
                "5b": ((0, -sign), (0, 2), 1, part),
                "6": ((2, 0), (2, -sign), 1, 0),
                "7a": ((1, -sign), (1, 2), 1, part),
                "7b": ((-1, -sign), (-1, 2), 1, part),
                "8": ((2, -sign), (2, 2), 1, part),
            }[stage]
            found.append((lane, one[0], one[1], one[2], sign, one[3]))
    return found


def rows_of(part):
    return (0, HALF) if part == 0 else ((0, HALF // 2) if part == 1 else (HALF // 2, HALF // 2))


def kernel(
    act_ref, w_ref, g_ref, u_ref, len_ref, wt_ref, out_ref,
    u, w, gb, pf, cs, cr, sb, rr, rb, rabs, ra, ab, acc,
    load_sem, xy_send, xy_recv, core_send, core_recv, rs_send, rs_recv,
    ag_send, ag_recv, fw_send, fw_recv, co_send, co_recv, az_send, az_recv, ac_send, ac_recv, out_sem,
):
    i, o = lax.axis_index("in"), lax.axis_index("out")
    z, c = lax.div(i, 2), lax.rem(i, 2)
    x, y = lax.div(o, 4), lax.rem(o, 4)
    width = ra.shape[1]
    half = rb.shape[2]

    def xy(axis, sign):
        if axis == 0:
            return (i, lax.rem(x + sign + 4, 4) * 4 + y)
        return (i, x * 4 + lax.rem(y + sign + 4, 4))

    def chip(d):
        return (lax.rem(z + d, 4) * 2 + c, o)

    other = (z * 2 + 1 - c, o)
    pending = []

    g_load = pltpu.make_async_copy(g_ref, gb.at[pl.ds(0, 2 * HALF)], load_sem.at[0])
    mine = pl.ds(pl.multiple_of(i * width, 128), width)
    a_load = pltpu.make_async_copy(act_ref, ab.at[:, mine], load_sem.at[1])
    u_load = pltpu.make_async_copy(u_ref, u, load_sem.at[2])
    w_load = pltpu.make_async_copy(w_ref, w, load_sem.at[3])
    for load in (g_load, a_load, u_load, w_load):
        load.start()

    peers = [xy(0, 1), xy(0, -1), xy(1, 1), xy(1, -1), chip(1), chip(2), chip(3), other]
    barrier = pltpu.get_barrier_semaphore()
    for peer in peers:
        pl.semaphore_signal(barrier, inc=1, device_id=peer, device_id_type=MESH)
    pl.semaphore_wait(barrier, len(peers))

    def remote(src, dst, send, recv, device):
        return pltpu.make_async_remote_copy(
            src_ref=src, dst_ref=dst, send_sem=send, recv_sem=recv, device_id=device, device_id_type=MESH
        )

    def token(lane, a, b):
        dx, dy = (b, a) if lane == 0 else (a, b)
        shard = lax.rem(x + dx + 4, 4) * 4 + lax.rem(y + dy + 4, 4)
        return shard * 2 * HALF + lane * HALF

    def xy_copy(kind, stage, at, arriving):
        lane, src, dst, axis, sign, part = moves(stage)[at]
        number = 4 * STAGES.index(stage) - 4 + at
        start, size = rows_of(part)
        if kind == 0:
            from_row, to_row, ref = OFFSET[(lane, *src)] + start, OFFSET[(lane, *dst)] + start, gb
        else:
            ref = ra
            from_row = pl.multiple_of(token(lane, *src) + start, 16)
            to_row = pl.multiple_of(token(lane, *dst) + start, 16) if arriving else from_row
        return remote(
            ref.at[pl.ds(from_row, size)], ref.at[pl.ds(to_row, size)],
            xy_send.at[kind, number], xy_recv.at[kind, number],
            xy(1 - axis if lane == 0 else axis, sign),
        )

    def issue(kind, *stages):
        for stage in stages:
            for at in range(4):
                copy = xy_copy(kind, stage, at, False)
                copy.start()
                pending.append(copy)

    def arrive(kind, *stages):
        for stage in stages:
            for at in range(4):
                xy_copy(kind, stage, at, True).wait_recv()

    own_cols = pl.ds(pl.multiple_of(c * half, 128), half)
    other_cols = pl.ds(pl.multiple_of((1 - c) * half, 128), half)

    def core_copy(q):
        row, m = GROUPS[q]
        return remote(cs.at[pl.ds(row, m)], cr.at[pl.ds(row, m)], core_send.at[q], core_recv.at[q], other)

    def s1(q):
        row, m = GROUPS[q]

        def tile(n, carry):
            cols = pl.ds(pl.multiple_of(n * 256, 256), 256)
            pf[pl.ds(row, m), cols] = jnp.dot(gb[pl.ds(row, m)], u[:, cols], preferred_element_type=jnp.float32)
            return carry

        lax.fori_loop(0, pf.shape[1] // 256, tile, 0)
        cs[pl.ds(row, m)] = pf[pl.ds(row, m), other_cols].astype(cs.dtype)
        copy = core_copy(q)
        copy.start()
        pending.append(copy)

    def rs_copy(q, d):
        row, m = GROUPS[q]
        n = m // 4
        there = lax.rem(z + d, 4)
        return remote(
            sb.at[pl.ds(pl.multiple_of(row + there * n, 16), n)], rr.at[d - 1, pl.ds(row // 4, n)],
            rs_send.at[q, d - 1], rs_recv.at[q, d - 1], chip(d),
        )

    def s2(q):
        row, m = GROUPS[q]
        core_copy(q).wait_recv()
        sb[pl.ds(row, m)] = (pf[pl.ds(row, m), own_cols] + cr[pl.ds(row, m)].astype(jnp.float32)).astype(sb.dtype)
        for d in (2, 1, 3):
            copy = rs_copy(q, d)
            copy.start()
            pending.append(copy)

    def piece(q, there):
        row, m = GROUPS[q]
        return pl.multiple_of(row + there * (m // 4), 16)

    def ag_copy(q, d, arriving):
        n = GROUPS[q][1] // 4
        at = piece(q, lax.rem(z - d + 4, 4) if arriving else z)
        block = rb.at[c, pl.ds(at, n)]
        return remote(block, block, ag_send.at[q, d - 1], ag_recv.at[q, d - 1], chip(d))

    def far(q):
        return GROUPS[q][1] < 128

    def s3(q):
        row, m = GROUPS[q]
        n = m // 4
        for d in (1, 2, 3):
            rs_copy(q, d).wait_recv()
        at = pl.ds(piece(q, z), n)
        total = pf[at, own_cols] + cr[at].astype(jnp.float32)
        for d in (1, 2, 3):
            total = total + rr[d - 1, pl.ds(row // 4, n)].astype(jnp.float32)
        rb[c, at] = total.astype(rb.dtype)
        for d in (2, 1, 3) if far(q) else (1, 3):
            copy = ag_copy(q, d, False)
            copy.start()
            pending.append(copy)

    def fw_copy(q, way, arriving):
        n = GROUPS[q][1] // 4
        first = n // 32 * 16
        start, size = (0, first) if way == 0 else (first, n - first)
        at = piece(q, lax.rem(z + 2, 4) if arriving else lax.rem(z + (3 if way == 0 else 1), 4)) + start
        block = rb.at[c, pl.ds(pl.multiple_of(at, 16), size)]
        return remote(block, block, fw_send.at[q, way], fw_recv.at[q, way], chip(1 if way == 0 else 3))

    def s3b(q):
        if far(q):
            return
        for d, way in ((1, 0), (3, 1)):
            ag_copy(q, d, True).wait_recv()
            copy = fw_copy(q, way, False)
            copy.start()
            pending.append(copy)

    def co_copy(q, arriving):
        row, m = GROUPS[q]
        block = rb.at[1 - c if arriving else c, pl.ds(row, m)]
        return remote(block, block, co_send.at[q], co_recv.at[q], other)

    def s4(q):
        if far(q):
            for d in (1, 2, 3):
                ag_copy(q, d, True).wait_recv()
        else:
            for way in (0, 1):
                fw_copy(q, way, True).wait_recv()
        copy = co_copy(q, False)
        copy.start()
        pending.append(copy)

    def s5(q):
        row, m = GROUPS[q]
        co_copy(q, True).wait_recv()
        for at in range(row // HALF, (row + m) // HALF):
            first = pl.multiple_of(token(*SLOTS[at]), 16)
            length = len_ref[lax.div(first, 4 * HALF)]
            position = lax.broadcasted_iota(jnp.int32, (HALF, half), 0) + lax.rem(first, 4 * HALF)
            for h in (0, 1):
                block = rb[h, pl.ds(at * HALF, HALF)].astype(jnp.float32)
                rabs[pl.ds(first, HALF), pl.ds(h * half, half)] = jnp.where(position < length, block, 0.0).astype(rabs.dtype)

    def az_copy(d, arriving):
        from_z = lax.rem(z - d + 4, 4) if arriving else z
        block = ab.at[:, pl.ds(pl.multiple_of((from_z * 2 + c) * width, 128), width)]
        return remote(block, block, az_send.at[d - 1], az_recv.at[d - 1], chip(d))

    def ac_copy(d, arriving):
        there = lax.rem(z + d, 4) * 2 + (1 - c if arriving else c)
        block = ab.at[:, pl.ds(pl.multiple_of(there * width, 128), width)]
        return remote(block, block, ac_send.at[d], ac_recv.at[d], other)

    def rotate_act():
        for d in range(4):
            ac_copy(d, True).wait_recv()
        w_load.wait()
        first = pl.multiple_of(o * 2 * HALF, 16)
        for start in range(0, width, 256):
            size = min(256, width - start)
            ra[pl.ds(first, 2 * HALF), pl.ds(start, size)] = jnp.dot(
                ab[...], w[:, pl.ds(start, size)], preferred_element_type=jnp.float32
            ).astype(ra.dtype)

    h0 = lax.div(y, 2)
    sequences = [
        x * 2 + h0, x * 2 + 1 - h0,
        lax.rem(x + 1, 4) * 2 + h0, lax.rem(x + 3, 4) * 2 + h0,
        lax.rem(x + 1, 4) * 2 + 1 - h0, lax.rem(x + 3, 4) * 2 + 1 - h0,
        lax.rem(x + 2, 4) * 2 + h0, lax.rem(x + 2, 4) * 2 + 1 - h0,
    ]
    weight_sum = wt_ref[0]
    for n in range(1, 8):
        weight_sum = weight_sum + wt_ref[n]
    weight_sum = weight_sum.astype(jnp.float32)
    tile_rows = 256

    def out_copy(j):
        rows = pl.ds(pl.multiple_of(j * tile_rows, 8), tile_rows)
        return pltpu.make_async_copy(acc.at[rows], out_ref.at[rows], out_sem.at[j])

    def final(batch, last):
        def tile(j, carry):
            cols = pl.ds(pl.multiple_of(j * tile_rows, tile_rows), tile_rows)
            total = None if batch[0] == 0 else acc[cols]
            for s in batch:
                rows = pl.ds(pl.multiple_of(sequences[s] * 128, 128), 128)
                block = lax.dot_general(
                    rabs[rows, cols], ra[rows], (((0,), (0,)), ((), ())), preferred_element_type=jnp.float32
                )
                term = wt_ref[sequences[s]].astype(jnp.float32) * block * block
                total = term if total is None else total + term
            if last:
                acc[cols] = total / weight_sum
                out_copy(j).start()
            else:
                acc[cols] = total
            return carry

        lax.fori_loop(0, acc.shape[0] // tile_rows, tile, 0)

    g_load.wait()
    issue(0, "1", "2")
    a_load.wait()
    for d in (2, 1, 3):
        copy = az_copy(d, False)
        copy.start()
        pending.append(copy)
    u_load.wait()

    arrive(0, "1")
    issue(0, "3a", "3b", "4b")
    s1(0)
    for d in (0, 1, 2, 3):
        if d:
            az_copy(4 - d, True).wait_recv()
        copy = ac_copy(d, False)
        copy.start()
        pending.append(copy)

    arrive(0, "2")
    issue(0, "5b")
    s2(0)
    s1(1)
    rotate_act()

    arrive(0, "3a")
    issue(0, "6")
    arrive(0, "3b")
    issue(0, "7a")
    s3(0)
    s2(1)
    s1(2)

    arrive(0, "4b")
    issue(0, "7b")
    arrive(0, "5b")
    s3b(0)
    s3(1)
    s2(2)
    s1(3)

    arrive(0, "6")
    issue(0, "8")
    issue(1, "1", "2")
    s4(0)
    s3b(1)
    s3(2)
    s2(3)
    s1(4)

    arrive(0, "7a", "7b")
    s5(0)
    s4(1)
    s3b(2)
    s3(3)
    s2(4)
    s1(5)

    arrive(0, "8")
    s1(6)
    s2(5)
    s3(4)
    s3b(3)
    s4(2)
    s5(1)

    s2(6)
    arrive(1, "1")
    issue(1, "3a", "3b", "4b")
    arrive(1, "2")
    issue(1, "5b")
    s3(5)
    s3b(4)
    s4(3)
    s5(2)

    s3(6)
    arrive(1, "3a")
    issue(1, "6")
    arrive(1, "3b")
    issue(1, "7a")
    s3b(5)
    s4(4)
    s5(3)

    arrive(1, "4b")
    issue(1, "7b")
    arrive(1, "5b")
    s4(5)
    s4(6)
    arrive(1, "6")
    issue(1, "8")
    final((0, 1, 2, 3), False)
    s5(4)
    s5(5)
    arrive(1, "7a", "7b")
    final((4, 5, 6), False)
    s5(6)
    arrive(1, "8")
    final((7,), True)

    for copy in pending:
        copy.wait_send()
    for j in range(acc.shape[0] // tile_rows):
        out_copy(j).wait()


def local(activations, act_basis, gradients, grad_basis, lengths, sample_weights):
    rows, wide = gradients.shape
    depth, cols = grad_basis.shape
    full, width = act_basis.shape
    tokens = 16 * rows
    groups = len(GROUPS)
    bf16, f32 = jnp.bfloat16, jnp.float32
    dma = pltpu.SemaphoreType.DMA
    anywhere = pl.BlockSpec(memory_space=pl.ANY)
    scalars = pl.BlockSpec(memory_space=pltpu.SMEM)
    return pl.pallas_call(
        kernel,
        out_shape=jax.ShapeDtypeStruct((cols, width), f32),
        in_specs=[anywhere] * 4 + [scalars] * 2,
        out_specs=anywhere,
        scratch_shapes=[
            pltpu.VMEM((depth, cols), bf16),
            pltpu.VMEM((full, width), bf16),
            pltpu.VMEM((tokens, wide), bf16),
            pltpu.VMEM((tokens, cols), f32),
            pltpu.VMEM((tokens, cols // 2), bf16),
            pltpu.VMEM((tokens, cols // 2), bf16),
            pltpu.VMEM((tokens, cols // 2), bf16),
            pltpu.VMEM((3, tokens // 4, cols // 2), bf16),
            pltpu.VMEM((2, tokens, cols // 2), bf16),
            pltpu.VMEM((tokens, cols), bf16),
            pltpu.VMEM((tokens, width), bf16),
            pltpu.VMEM((rows, full), bf16),
            pltpu.VMEM((cols, width), f32),
            dma((4,)),
            dma((2, 40)), dma((2, 40)),
            dma((groups,)), dma((groups,)),
            dma((groups, 3)), dma((groups, 3)),
            dma((groups, 3)), dma((groups, 3)),
            dma((groups, 2)), dma((groups, 2)),
            dma((groups,)), dma((groups,)),
            dma((3,)), dma((3,)),
            dma((4,)), dma((4,)),
            dma((cols // 256,)),
        ],
        compiler_params=pltpu.CompilerParams(
            collective_id=0, has_side_effects=True, vmem_limit_bytes=56 * 1024 * 1024
        ),
    )(activations, act_basis, gradients, grad_basis, lengths, sample_weights)


def solution(mesh):
    in_specs = (P("out", "in"), P(None, "in"), P("out", "in"), P("in", "out"), P(), P())
    return jax.shard_map(local, mesh=mesh, in_specs=in_specs, out_specs=P("out", "in"), check_vma=False)
```

time: 284 us -> 69.5 us (0.24)
  waiting for transfers between devices: 105 us -> 0 us
  blocking collectives: 101 us -> 0 us
  Pallas kernels: 0 us -> 65 us
  matrix products: 48.9 us -> 0 us
  between operations: 13.1 us -> 0.01 us
  other arithmetic: 8.8 us -> 0 us
    all_gather x3 -> x0, waiting for transfers between devices: 103 us -> none  [the longest x1 56 us: local(): lax.all_gather(gradients, 'out', axis=0, tiled=True)]
    psum x1 -> x0, blocking collectives: 101 us -> none  [local(): rot_rows = lax.psum(partial_rot, 'in').astype(jnp.bfloat16)]
    pallas_call x0 -> x1, Pallas kernels: none -> 65 us  [local(): pl.pallas_call(kernel, out_shape=jax.ShapeDtypeStruct((cols, width), f32)...]
    dot_general x10 -> x0, matrix products: 48.9 us -> none  [the longest x8 23 us: accumulate(): lax.dot_general(grad_one, act_one, (((0,), (0,)), ((), ())), preferred_el...]
    dynamic_slice x8 -> x0, local copies, waits for them, and re-layouts: 4.76 us -> none  [local(): lax.scan(accumulate, start_total, (grad_seq, act_seq, weights))]
    unnamed x0 -> x1, local copies, waits for them, and re-layouts: none -> 3.84 us
    mul x1 -> x0, other arithmetic: 3.47 us -> none  [local(): rot_rows.reshape(seq_count, slot_count, rot_rows.shape[1])]
  transfers between devices with their start and end apart: 3 -> 0, of which waited for: 2 -> 0; matrix products, arithmetic and copies ran while one was open for 7% -> 0% of each run, Pallas kernels for 0% -> 0%
where the time goes in v1:
time: 69.5 us; the launch traced here: 68.8 us
  Pallas kernels  65 us (94%)
  local copies, waits for them, and re-layouts  3.84 us (6%)
    pallas_call x1, Pallas kernels, local(): pl.pallas_call(kernel, out_shape=jax.ShapeDtypeStruct((cols, width), f32)...  65 us
    unnamed x1, local copies, waits for them, and re-layouts  3.84 us

profile of v1, /device:TPU:1, one launch (start us, length us, event | category | flops | bytes accessed | tf_op | source)
XLA Modules:
  0.0 68.8 jit_solution(1044909239091796922)
XLA Ops:
  0.0 65.0 %shard_map.64 = f32[1280,640]{1,0:T(8,128)} custom-call(bf16[64,640]{1,0:T(8,128)(2,1)} %act_ref.1, bf16[5120,640]{1,0:T(8,128)(2,1)} %w_ref.1, bf16[64,2560]{1,0:T(8,128)(2,1)} %g_ref.1, bf16[2560,1280]{1,0:T(8,128)(2,1)} %u_ref.1, s32[8]{0:T(128)} %len_ref.1, s32[8]{0:T(128)} %wt_ref.1), custom_call_target="tpu_custom_call" | custom-call | tf_op jit(solution)/shard_map/pallas_call | solution.py:417
  65.0 3.8 %copy.8 = f32[1280,640]{1,0:T(8,128)} copy(f32[1280,640]{1,0:T(8,128)} %shard_map.64) | data formatting | bytes 6553600

commit v2 on v1

--- a/solution.py
+++ b/solution.py
@@ -128,26 +128,27 @@
             for at in range(4):
                 xy_copy(kind, stage, at, True).wait_recv()
 
-    own_cols = pl.ds(pl.multiple_of(c * half, 128), half)
-    other_cols = pl.ds(pl.multiple_of((1 - c) * half, 128), half)
-
     def core_copy(q):
         row, m = GROUPS[q]
         return remote(cs.at[pl.ds(row, m)], cr.at[pl.ds(row, m)], core_send.at[q], core_recv.at[q], other)
 
     def s1(q):
         row, m = GROUPS[q]
-
-        def tile(n, carry):
-            cols = pl.ds(pl.multiple_of(n * 256, 256), 256)
-            pf[pl.ds(row, m), cols] = jnp.dot(gb[pl.ds(row, m)], u[:, cols], preferred_element_type=jnp.float32)
+        rows = pl.ds(row, m)
+
+        def side(n, carry):
+            cols = pl.ds(pl.multiple_of(lax.rem(1 - c + n, 2) * half, 128), half)
+            pf[rows] = jnp.dot(gb[rows], u[:, cols], preferred_element_type=jnp.float32)
+
+            @pl.when(n == 0)
+            def _():
+                cs[rows] = pf[rows].astype(cs.dtype)
+                core_copy(q).start()
+
             return carry
 
-        lax.fori_loop(0, pf.shape[1] // 256, tile, 0)
-        cs[pl.ds(row, m)] = pf[pl.ds(row, m), other_cols].astype(cs.dtype)
-        copy = core_copy(q)
-        copy.start()
-        pending.append(copy)
+        lax.fori_loop(0, 2, side, 0)
+        pending.append(core_copy(q))
 
     def rs_copy(q, d):
         row, m = GROUPS[q]
@@ -161,7 +162,7 @@
     def s2(q):
         row, m = GROUPS[q]
         core_copy(q).wait_recv()
-        sb[pl.ds(row, m)] = (pf[pl.ds(row, m), own_cols] + cr[pl.ds(row, m)].astype(jnp.float32)).astype(sb.dtype)
+        sb[pl.ds(row, m)] = (pf[pl.ds(row, m)] + cr[pl.ds(row, m)].astype(jnp.float32)).astype(sb.dtype)
         for d in (2, 1, 3):
             copy = rs_copy(q, d)
             copy.start()
@@ -178,7 +179,7 @@
         return remote(block, block, ag_send.at[q, d - 1], ag_recv.at[q, d - 1], chip(d))
 
     def far(q):
-        return GROUPS[q][1] < 128
+        return q >= 5
 
     def s3(q):
         row, m = GROUPS[q]
@@ -186,7 +187,7 @@
         for d in (1, 2, 3):
             rs_copy(q, d).wait_recv()
         at = pl.ds(piece(q, z), n)
-        total = pf[at, own_cols] + cr[at].astype(jnp.float32)
+        total = pf[at] + cr[at].astype(jnp.float32)
         for d in (1, 2, 3):
             total = total + rr[d - 1, pl.ds(row // 4, n)].astype(jnp.float32)
         rb[c, at] = total.astype(rb.dtype)
@@ -228,16 +229,20 @@
         copy.start()
         pending.append(copy)
 
-    def s5(q):
-        row, m = GROUPS[q]
-        co_copy(q, True).wait_recv()
+    def side_of(n):
+        return c if n == 0 else 1 - c
+
+    def s5(q, n):
+        row, m = GROUPS[q]
+        if n == 1:
+            co_copy(q, True).wait_recv()
+        h = side_of(n)
         for at in range(row // HALF, (row + m) // HALF):
             first = pl.multiple_of(token(*SLOTS[at]), 16)
             length = len_ref[lax.div(first, 4 * HALF)]
             position = lax.broadcasted_iota(jnp.int32, (HALF, half), 0) + lax.rem(first, 4 * HALF)
-            for h in (0, 1):
-                block = rb[h, pl.ds(at * HALF, HALF)].astype(jnp.float32)
-                rabs[pl.ds(first, HALF), pl.ds(h * half, half)] = jnp.where(position < length, block, 0.0).astype(rabs.dtype)
+            block = rb[h, pl.ds(at * HALF, HALF)].astype(jnp.float32)
+            rabs[h, pl.ds(first, HALF)] = jnp.where(position < length, block, 0.0).astype(rabs.dtype)
 
     def az_copy(d, arriving):
         from_z = lax.rem(z - d + 4, 4) if arriving else z
@@ -271,137 +276,133 @@
     for n in range(1, 8):
         weight_sum = weight_sum + wt_ref[n]
     weight_sum = weight_sum.astype(jnp.float32)
-    tile_rows = 256
-
-    def out_copy(j):
-        rows = pl.ds(pl.multiple_of(j * tile_rows, 8), tile_rows)
-        return pltpu.make_async_copy(acc.at[rows], out_ref.at[rows], out_sem.at[j])
-
-    def final(batch, last):
-        def tile(j, carry):
-            cols = pl.ds(pl.multiple_of(j * tile_rows, tile_rows), tile_rows)
-            total = None if batch[0] == 0 else acc[cols]
-            for s in batch:
-                rows = pl.ds(pl.multiple_of(sequences[s] * 128, 128), 128)
-                block = lax.dot_general(
-                    rabs[rows, cols], ra[rows], (((0,), (0,)), ((), ())), preferred_element_type=jnp.float32
-                )
-                term = wt_ref[sequences[s]].astype(jnp.float32) * block * block
-                total = term if total is None else total + term
-            if last:
-                acc[cols] = total / weight_sum
-                out_copy(j).start()
-            else:
-                acc[cols] = total
-            return carry
-
-        lax.fori_loop(0, acc.shape[0] // tile_rows, tile, 0)
+    def out_copy(n):
+        rows = pl.ds(pl.multiple_of(side_of(n) * half, 8), half)
+        return pltpu.make_async_copy(acc.at[rows], out_ref.at[rows], out_sem.at[n])
+
+    def final(batch, n):
+        h = side_of(n)
+        cols = pl.ds(pl.multiple_of(h * half, 8), half)
+        for s in batch:
+            rows = pl.ds(pl.multiple_of(sequences[s] * 128, 128), 128)
+            block = lax.dot_general(
+                rabs[h, rows], ra[rows], (((0,), (0,)), ((), ())), preferred_element_type=jnp.float32
+            )
+            term = wt_ref[sequences[s]].astype(jnp.float32) * block * block
+            total = term if s == 0 else acc[cols] + term
+            acc[cols] = total / weight_sum if s == 7 else total
+        if batch[-1] == 7:
+            out_copy(n).start()
+
+    def first_act():
+        a_load.wait()
+        for d in (2, 1, 3):
+            copy = az_copy(d, False)
+            copy.start()
+            pending.append(copy)
+
+    def swap_act():
+        for d in (0, 1, 2, 3):
+            if d:
+                az_copy(4 - d, True).wait_recv()
+            copy = ac_copy(d, False)
+            copy.start()
+            pending.append(copy)
 
     g_load.wait()
     issue(0, "1", "2")
-    a_load.wait()
-    for d in (2, 1, 3):
-        copy = az_copy(d, False)
-        copy.start()
-        pending.append(copy)
+    first_act()
     u_load.wait()
-
     arrive(0, "1")
     issue(0, "3a", "3b", "4b")
     s1(0)
-    for d in (0, 1, 2, 3):
-        if d:
-            az_copy(4 - d, True).wait_recv()
-        copy = ac_copy(d, False)
-        copy.start()
-        pending.append(copy)
-
+    swap_act()
+    s2(0)
     arrive(0, "2")
     issue(0, "5b")
-    s2(0)
     s1(1)
-    rotate_act()
-
     arrive(0, "3a")
     issue(0, "6")
+    rotate_act()
+    s2(1)
+    s3(0)
     arrive(0, "3b")
     issue(0, "7a")
-    s3(0)
-    s2(1)
     s1(2)
-
+    s2(2)
+    s3(1)
+    s3b(0)
     arrive(0, "4b")
     issue(0, "7b")
     arrive(0, "5b")
-    s3b(0)
-    s3(1)
-    s2(2)
     s1(3)
-
+    s2(3)
+    s3(2)
     arrive(0, "6")
     issue(0, "8")
     issue(1, "1", "2")
+    s1(4)
+    s3b(1)
     s4(0)
-    s3b(1)
-    s3(2)
-    s2(3)
-    s1(4)
-
+    s5(0, 0)
+    s2(4)
     arrive(0, "7a", "7b")
-    s5(0)
-    s4(1)
-    s3b(2)
+    s1(5)
     s3(3)
-    s2(4)
-    s1(5)
-
+    s2(5)
     arrive(0, "8")
     s1(6)
-    s2(5)
-    s3(4)
-    s3b(3)
-    s4(2)
-    s5(1)
-
+    s3b(2)
     s2(6)
+    s4(1)
     arrive(1, "1")
     issue(1, "3a", "3b", "4b")
+    s3(4)
     arrive(1, "2")
     issue(1, "5b")
-    s3(5)
-    s3b(4)
-    s4(3)
-    s5(2)
-
-    s3(6)
+    s5(1, 0)
+    s5(0, 1)
+    s3b(3)
+    s5(1, 1)
     arrive(1, "3a")
     issue(1, "6")
     arrive(1, "3b")
     issue(1, "7a")
-    s3b(5)
-    s4(4)
-    s5(3)
-
+    s3(5)
     arrive(1, "4b")
     issue(1, "7b")
+    s4(2)
+    s5(2, 0)
+    s3(6)
+    s5(2, 1)
+    s3b(4)
+    s4(3)
+    s5(3, 0)
     arrive(1, "5b")
-    s4(5)
-    s4(6)
     arrive(1, "6")
     issue(1, "8")
-    final((0, 1, 2, 3), False)
-    s5(4)
-    s5(5)
+    final((0, 1, 2, 3), 0)
+    s5(3, 1)
+    final((0, 1, 2, 3), 1)
+    s4(5)
+    s5(5, 0)
+    s4(4)
+    s5(4, 0)
+    s4(6)
+    s5(6, 0)
     arrive(1, "7a", "7b")
-    final((4, 5, 6), False)
-    s5(6)
+    final((4, 5, 6), 0)
     arrive(1, "8")
-    final((7,), True)
+    final((7,), 0)
+    s5(5, 1)
+    s5(4, 1)
+    s5(6, 1)
+    final((4, 5, 6, 7), 1)
 
     for copy in pending:
         copy.wait_send()
-    for j in range(acc.shape[0] // tile_rows):
-        out_copy(j).wait()
+    for n in (0, 1):
+        out_copy(n).wait()
 
 
 def local(activations, act_basis, gradients, grad_basis, lengths, sample_weights):
@@ -423,13 +424,13 @@
             pltpu.VMEM((depth, cols), bf16),
             pltpu.VMEM((full, width), bf16),
             pltpu.VMEM((tokens, wide), bf16),
-            pltpu.VMEM((tokens, cols), f32),
+            pltpu.VMEM((tokens, cols // 2), f32),
             pltpu.VMEM((tokens, cols // 2), bf16),
             pltpu.VMEM((tokens, cols // 2), bf16),
             pltpu.VMEM((tokens, cols // 2), bf16),
             pltpu.VMEM((3, tokens // 4, cols // 2), bf16),
             pltpu.VMEM((2, tokens, cols // 2), bf16),
-            pltpu.VMEM((tokens, cols), bf16),
+            pltpu.VMEM((2, tokens, cols // 2), bf16),
             pltpu.VMEM((tokens, width), bf16),
             pltpu.VMEM((rows, full), bf16),
             pltpu.VMEM((cols, width), f32),
@@ -442,7 +443,7 @@
             dma((groups,)), dma((groups,)),
             dma((3,)), dma((3,)),
             dma((4,)), dma((4,)),
-            dma((cols // 256,)),
+            dma((2,)),
         ],
         compiler_params=pltpu.CompilerParams(
             collective_id=0, has_side_effects=True, vmem_limit_bytes=56 * 1024 * 1024

time: 69.5 us -> 59.6 us (0.86)
  Pallas kernels: 65 us -> 55.6 us
    pallas_call x1, Pallas kernels: 65 us -> 55.6 us  [local(): pl.pallas_call(kernel, out_shape=jax.ShapeDtypeStruct((cols, width), f32)...]
where the time goes in v2:
time: 59.6 us; the launch traced here: 59.4 us
  Pallas kernels  55.6 us (93%)
  local copies, waits for them, and re-layouts  3.84 us (6%)
    pallas_call x1, Pallas kernels, local(): pl.pallas_call(kernel, out_shape=jax.ShapeDtypeStruct((cols, width), f32)...  55.6 us
    unnamed x1, local copies, waits for them, and re-layouts  3.84 us

profile of v2, /device:TPU:1, one launch (start us, length us, event | category | flops | bytes accessed | tf_op | source)
XLA Modules:
  0.0 59.4 jit_solution(17595766793718228266)
XLA Ops:
  0.0 55.6 %shard_map.64 = f32[1280,640]{1,0:T(8,128)} custom-call(bf16[64,640]{1,0:T(8,128)(2,1)} %act_ref.1, bf16[5120,640]{1,0:T(8,128)(2,1)} %w_ref.1, bf16[64,2560]{1,0:T(8,128)(2,1)} %g_ref.1, bf16[2560,1280]{1,0:T(8,128)(2,1)} %u_ref.1, s32[8]{0:T(128)} %len_ref.1, s32[8]{0:T(128)} %wt_ref.1), custom_call_target="tpu_custom_call" | custom-call | tf_op jit(solution)/shard_map/pallas_call | solution.py:418
  55.6 3.8 %copy.8 = f32[1280,640]{1,0:T(8,128)} copy(f32[1280,640]{1,0:T(8,128)} %shard_map.64) | data formatting | bytes 6553600

commit v3 on v2

--- a/solution.py
+++ b/solution.py
@@ -54,8 +54,8 @@
 
 
 def kernel(
-    act_ref, w_ref, g_ref, u_ref, len_ref, wt_ref, out_ref,
-    u, w, gb, pf, cs, cr, sb, rr, rb, rabs, ra, ab, acc,
+    act_ref, w_ref, g_ref, u_ref, len_hbm, wt_hbm, out_ref,
+    u, w, gb, pf, cs, cr, sb, rr, rb, rabs, ra, ab, acc, len_ref, wt_ref,
     load_sem, xy_send, xy_recv, core_send, core_recv, rs_send, rs_recv,
     ag_send, ag_recv, fw_send, fw_recv, co_send, co_recv, az_send, az_recv, ac_send, ac_recv, out_sem,
 ):
@@ -81,7 +81,9 @@
     a_load = pltpu.make_async_copy(act_ref, ab.at[:, mine], load_sem.at[1])
     u_load = pltpu.make_async_copy(u_ref, u, load_sem.at[2])
     w_load = pltpu.make_async_copy(w_ref, w, load_sem.at[3])
-    for load in (g_load, a_load, u_load, w_load):
+    len_load = pltpu.make_async_copy(len_hbm, len_ref, load_sem.at[4])
+    wt_load = pltpu.make_async_copy(wt_hbm, wt_ref, load_sem.at[5])
+    for load in (g_load, a_load, u_load, w_load, len_load, wt_load):
         load.start()
 
     peers = [xy(0, 1), xy(0, -1), xy(1, 1), xy(1, -1), chip(1), chip(2), chip(3), other]
@@ -116,12 +118,14 @@
             xy(1 - axis if lane == 0 else axis, sign),
         )
 
-    def issue(kind, *stages):
+    def issue(kind, *stages, start=True, record=True):
         for stage in stages:
             for at in range(4):
                 copy = xy_copy(kind, stage, at, False)
-                copy.start()
-                pending.append(copy)
+                if start:
+                    copy.start()
+                if record:
+                    pending.append(copy)
 
     def arrive(kind, *stages):
         for stage in stages:
@@ -132,7 +136,7 @@
         row, m = GROUPS[q]
         return remote(cs.at[pl.ds(row, m)], cr.at[pl.ds(row, m)], core_send.at[q], core_recv.at[q], other)
 
-    def s1(q):
+    def s1(q, between=None):
         row, m = GROUPS[q]
         rows = pl.ds(row, m)
 
@@ -144,6 +148,8 @@
             def _():
                 cs[rows] = pf[rows].astype(cs.dtype)
                 core_copy(q).start()
+                if between is not None:
+                    between()
 
             return carry
 
@@ -272,27 +278,37 @@
         lax.rem(x + 1, 4) * 2 + 1 - h0, lax.rem(x + 3, 4) * 2 + 1 - h0,
         lax.rem(x + 2, 4) * 2 + h0, lax.rem(x + 2, 4) * 2 + 1 - h0,
     ]
-    weight_sum = wt_ref[0]
-    for n in range(1, 8):
-        weight_sum = weight_sum + wt_ref[n]
-    weight_sum = weight_sum.astype(jnp.float32)
-    def out_copy(n):
-        rows = pl.ds(pl.multiple_of(side_of(n) * half, 8), half)
-        return pltpu.make_async_copy(acc.at[rows], out_ref.at[rows], out_sem.at[n])
+    def weight_sum():
+        total = wt_ref[0]
+        for n in range(1, 8):
+            total = total + wt_ref[n]
+        return total.astype(jnp.float32)
+
+    pieces = [(0, 0, half), (1, 0, 256), (1, 256, 256), (1, 512, half - 512)]
+
+    def out_copy(number):
+        n, start, size = pieces[number]
+        rows = pl.ds(pl.multiple_of(side_of(n) * half + start, 8), size)
+        return pltpu.make_async_copy(acc.at[rows], out_ref.at[rows], out_sem.at[number])
 
     def final(batch, n):
+        last = batch[-1] == 7
         h = side_of(n)
-        cols = pl.ds(pl.multiple_of(h * half, 8), half)
-        for s in batch:
-            rows = pl.ds(pl.multiple_of(sequences[s] * 128, 128), 128)
-            block = lax.dot_general(
-                rabs[h, rows], ra[rows], (((0,), (0,)), ((), ())), preferred_element_type=jnp.float32
-            )
-            term = wt_ref[sequences[s]].astype(jnp.float32) * block * block
-            total = term if s == 0 else acc[cols] + term
-            acc[cols] = total / weight_sum if s == 7 else total
-        if batch[-1] == 7:
-            out_copy(n).start()
+        for number, (side, start, size) in enumerate(pieces if last else [(n, 0, half)]):
+            if side != n:
+                continue
+            out = pl.ds(pl.multiple_of(h * half + start, 8), size)
+            for s in batch:
+                rows = pl.ds(pl.multiple_of(sequences[s] * 128, 128), 128)
+                block = lax.dot_general(
+                    rabs[h, rows, pl.ds(start, size)], ra[rows], (((0,), (0,)), ((), ())),
+                    preferred_element_type=jnp.float32,
+                )
+                term = wt_ref[sequences[s]].astype(jnp.float32) * block * block
+                total = term if s == 0 else acc[out] + term
+                acc[out] = total / weight_sum() if s == 7 else total
+            if last:
+                out_copy(number).start()
 
     def first_act():
         a_load.wait()
@@ -343,6 +359,8 @@
     issue(1, "1", "2")
     s1(4)
     s3b(1)
+    len_load.wait()
+    wt_load.wait()
     s4(0)
     s5(0, 0)
     s2(4)
@@ -397,12 +415,13 @@
     s5(5, 1)
     s5(4, 1)
     s5(6, 1)
-    final((4, 5, 6, 7), 1)
+    final((4, 5, 6), 1)
+    final((7,), 1)
 
     for copy in pending:
         copy.wait_send()
-    for n in (0, 1):
-        out_copy(n).wait()
+    for number in range(len(pieces)):
+        out_copy(number).wait()
 
 
 def local(activations, act_basis, gradients, grad_basis, lengths, sample_weights):
@@ -414,11 +433,10 @@
     bf16, f32 = jnp.bfloat16, jnp.float32
     dma = pltpu.SemaphoreType.DMA
     anywhere = pl.BlockSpec(memory_space=pl.ANY)
-    scalars = pl.BlockSpec(memory_space=pltpu.SMEM)
     return pl.pallas_call(
         kernel,
         out_shape=jax.ShapeDtypeStruct((cols, width), f32),
-        in_specs=[anywhere] * 4 + [scalars] * 2,
+        in_specs=[anywhere] * 6,
         out_specs=anywhere,
         scratch_shapes=[
             pltpu.VMEM((depth, cols), bf16),
@@ -434,7 +452,9 @@
             pltpu.VMEM((tokens, width), bf16),
             pltpu.VMEM((rows, full), bf16),
             pltpu.VMEM((cols, width), f32),
-            dma((4,)),
+            pltpu.SMEM((8,), jnp.int32),
+            pltpu.SMEM((8,), jnp.int32),
+            dma((6,)),
             dma((2, 40)), dma((2, 40)),
             dma((groups,)), dma((groups,)),
             dma((groups, 3)), dma((groups, 3)),
@@ -443,7 +463,7 @@
             dma((groups,)), dma((groups,)),
             dma((3,)), dma((3,)),
             dma((4,)), dma((4,)),
-            dma((2,)),
+            dma((4,)),
         ],
         compiler_params=pltpu.CompilerParams(
             collective_id=0, has_side_effects=True, vmem_limit_bytes=56 * 1024 * 1024

time: 59.6 us -> 58.8 us (0.987)
  Pallas kernels: 55.6 us -> 54.8 us
    pallas_call x1, Pallas kernels: 55.6 us -> 54.8 us  [local(): pl.pallas_call(kernel, out_shape=jax.ShapeDtypeStruct((cols, width), f32)...]
where the time goes in v3:
time: 58.8 us; the launch traced here: 58.7 us
  Pallas kernels  54.8 us (93%)
  local copies, waits for them, and re-layouts  3.84 us (7%)
    pallas_call x1, Pallas kernels, local(): pl.pallas_call(kernel, out_shape=jax.ShapeDtypeStruct((cols, width), f32)...  54.8 us
    unnamed x1, local copies, waits for them, and re-layouts  3.84 us

profile of v3, /device:TPU:1, one launch (start us, length us, event | category | flops | bytes accessed | tf_op | source)
XLA Modules:
  0.0 58.7 jit_solution(17367973944709535486)
XLA Ops:
  0.0 54.8 %shard_map.64 = f32[1280,640]{1,0:T(8,128)} custom-call(bf16[64,640]{1,0:T(8,128)(2,1)} %act_ref.1, bf16[5120,640]{1,0:T(8,128)(2,1)} %w_ref.1, bf16[64,2560]{1,0:T(8,128)(2,1)} %g_ref.1, bf16[2560,1280]{1,0:T(8,128)(2,1)} %u_ref.1, s32[8]{0:T(128)} %len_hbm.1, s32[8]{0:T(128)} %wt_hbm.1), custom_call_target="tpu_custom_call" | custom-call | tf_op jit(solution)/shard_map/pallas_call | solution.py:436
  54.8 3.8 %copy.8 = f32[1280,640]{1,0:T(8,128)} copy(f32[1280,640]{1,0:T(8,128)} %shard_map.64) | data formatting | bytes 6553600

commit v4 on v3

--- a/solution.py
+++ b/solution.py
@@ -25,7 +25,7 @@
 }
 SLOTS = [(lane, a, b) for stage in STAGES for lane in (0, 1) for a, b in BRINGS[stage]]
 OFFSET = {slot: HALF * at for at, slot in enumerate(SLOTS)}
-GROUPS = [(0, 192), (192, 128), (320, 192), (512, 192), (704, 128), (832, 128), (960, 64)]
+GROUPS = [(0, 64), (64, 128), (192, 128), (320, 192), (512, 192), (704, 128), (832, 128), (960, 64)]
 
 
 def moves(stage):
@@ -83,7 +83,7 @@
     w_load = pltpu.make_async_copy(w_ref, w, load_sem.at[3])
     len_load = pltpu.make_async_copy(len_hbm, len_ref, load_sem.at[4])
     wt_load = pltpu.make_async_copy(wt_hbm, wt_ref, load_sem.at[5])
-    for load in (g_load, a_load, u_load, w_load, len_load, wt_load):
+    for load in (g_load, a_load, u_load, len_load, wt_load):
         load.start()
 
     peers = [xy(0, 1), xy(0, -1), xy(1, 1), xy(1, -1), chip(1), chip(2), chip(3), other]
@@ -185,7 +185,7 @@
         return remote(block, block, ag_send.at[q, d - 1], ag_recv.at[q, d - 1], chip(d))
 
     def far(q):
-        return q >= 5
+        return q >= 6 or q == 0
 
     def s3(q):
         row, m = GROUPS[q]
@@ -329,92 +329,99 @@
     issue(0, "1", "2")
     first_act()
     u_load.wait()
+    w_load.start()
+    s1(0)
+    s2(0)
     arrive(0, "1")
     issue(0, "3a", "3b", "4b")
-    s1(0)
+    s1(1)
     swap_act()
-    s2(0)
+    s3(0)
+    s2(1)
     arrive(0, "2")
     issue(0, "5b")
-    s1(1)
+    s1(2)
     arrive(0, "3a")
     issue(0, "6")
     rotate_act()
-    s2(1)
-    s3(0)
+    s4(0)
+    s2(2)
+    s3(1)
     arrive(0, "3b")
     issue(0, "7a")
-    s1(2)
-    s2(2)
-    s3(1)
-    s3b(0)
+    s1(3)
+    s2(3)
+    s3(2)
+    s3b(1)
     arrive(0, "4b")
     issue(0, "7b")
     arrive(0, "5b")
-    s1(3)
-    s2(3)
-    s3(2)
+    s1(4)
+    s2(4)
+    s3(3)
     arrive(0, "6")
     issue(0, "8")
     issue(1, "1", "2")
-    s1(4)
-    s3b(1)
+    s1(5)
+    s3b(2)
+    s4(1)
     len_load.wait()
     wt_load.wait()
-    s4(0)
     s5(0, 0)
-    s2(4)
+    s5(0, 1)
+    s5(1, 0)
+    s2(5)
     arrive(0, "7a", "7b")
-    s1(5)
-    s3(3)
-    s2(5)
+    s1(6)
+    s3(4)
+    s2(6)
     arrive(0, "8")
-    s1(6)
-    s3b(2)
-    s2(6)
-    s4(1)
+    s1(7)
+    s3b(3)
+    s2(7)
+    s4(2)
     arrive(1, "1")
     issue(1, "3a", "3b", "4b")
-    s3(4)
+    s3(5)
     arrive(1, "2")
     issue(1, "5b")
-    s5(1, 0)
-    s5(0, 1)
-    s3b(3)
+    s5(2, 0)
     s5(1, 1)
+    s3b(4)
+    s5(2, 1)
     arrive(1, "3a")
     issue(1, "6")
     arrive(1, "3b")
     issue(1, "7a")
-    s3(5)
+    s3(6)
     arrive(1, "4b")
     issue(1, "7b")
-    s4(2)
-    s5(2, 0)
-    s3(6)
-    s5(2, 1)
-    s3b(4)
     s4(3)
     s5(3, 0)
+    s3(7)
+    s5(3, 1)
+    s3b(5)
+    s4(4)
+    s5(4, 0)
     arrive(1, "5b")
     arrive(1, "6")
     issue(1, "8")
     final((0, 1, 2, 3), 0)
-    s5(3, 1)
+    s5(4, 1)
     final((0, 1, 2, 3), 1)
+    s4(6)
+    s5(6, 0)
     s4(5)
     s5(5, 0)
-    s4(4)
-    s5(4, 0)
-    s4(6)
-    s5(6, 0)
+    s4(7)
+    s5(7, 0)
     arrive(1, "7a", "7b")
     final((4, 5, 6), 0)
     arrive(1, "8")
     final((7,), 0)
+    s5(6, 1)
     s5(5, 1)
-    s5(4, 1)
-    s5(6, 1)
+    s5(7, 1)
     final((4, 5, 6), 1)
     final((7,), 1)
 

time: 58.8 us -> 59 us (level)
  no operation moved by 1% of the time
where the time goes in v4:
time: 59 us; the launch traced here: 58.8 us
  Pallas kernels  55 us (93%)
  local copies, waits for them, and re-layouts  3.84 us (7%)
    pallas_call x1, Pallas kernels, local(): pl.pallas_call(kernel, out_shape=jax.ShapeDtypeStruct((cols, width), f32)...  55 us
    unnamed x1, local copies, waits for them, and re-layouts  3.84 us

profile of v4, /device:TPU:1, one launch (start us, length us, event | category | flops | bytes accessed | tf_op | source)
XLA Modules:
  0.0 58.8 jit_solution(14232190091493470173)
XLA Ops:
  0.0 55.0 %shard_map.64 = f32[1280,640]{1,0:T(8,128)} custom-call(bf16[64,640]{1,0:T(8,128)(2,1)} %act_ref.1, bf16[5120,640]{1,0:T(8,128)(2,1)} %w_ref.1, bf16[64,2560]{1,0:T(8,128)(2,1)} %g_ref.1, bf16[2560,1280]{1,0:T(8,128)(2,1)} %u_ref.1, s32[8]{0:T(128)} %len_hbm.1, s32[8]{0:T(128)} %wt_hbm.1), custom_call_target="tpu_custom_call" | custom-call | tf_op jit(solution)/shard_map/pallas_call | solution.py:443
  55.0 3.8 %copy.8 = f32[1280,640]{1,0:T(8,128)} copy(f32[1280,640]{1,0:T(8,128)} %shard_map.64) | data formatting | bytes 6553600

commit v5 on v3

--- a/solution.py
+++ b/solution.py
@@ -83,13 +83,14 @@
     w_load = pltpu.make_async_copy(w_ref, w, load_sem.at[3])
     len_load = pltpu.make_async_copy(len_hbm, len_ref, load_sem.at[4])
     wt_load = pltpu.make_async_copy(wt_hbm, wt_ref, load_sem.at[5])
-    for load in (g_load, a_load, u_load, w_load, len_load, wt_load):
-        load.start()
+    g_load.start()
 
     peers = [xy(0, 1), xy(0, -1), xy(1, 1), xy(1, -1), chip(1), chip(2), chip(3), other]
     barrier = pltpu.get_barrier_semaphore()
     for peer in peers:
         pl.semaphore_signal(barrier, inc=1, device_id=peer, device_id_type=MESH)
+    for load in (a_load, u_load, w_load, len_load, wt_load):
+        load.start()
     pl.semaphore_wait(barrier, len(peers))
 
     def remote(src, dst, send, recv, device):

time: 58.8 us -> 58.8 us (level)
  no operation moved by 1% of the time
where the time goes in v5:
time: 58.8 us; the launch traced here: 58.7 us
  Pallas kernels  54.8 us (93%)
  local copies, waits for them, and re-layouts  3.84 us (7%)
    pallas_call x1, Pallas kernels, local(): pl.pallas_call(kernel, out_shape=jax.ShapeDtypeStruct((cols, width), f32)...  54.8 us
    unnamed x1, local copies, waits for them, and re-layouts  3.84 us

profile of v5, /device:TPU:1, one launch (start us, length us, event | category | flops | bytes accessed | tf_op | source)
XLA Modules:
  0.0 58.7 jit_solution(12842159461113280864)
XLA Ops:
  0.0 54.8 %shard_map.64 = f32[1280,640]{1,0:T(8,128)} custom-call(bf16[64,640]{1,0:T(8,128)(2,1)} %act_ref.1, bf16[5120,640]{1,0:T(8,128)(2,1)} %w_ref.1, bf16[64,2560]{1,0:T(8,128)(2,1)} %g_ref.1, bf16[2560,1280]{1,0:T(8,128)(2,1)} %u_ref.1, s32[8]{0:T(128)} %len_hbm.1, s32[8]{0:T(128)} %wt_hbm.1), custom_call_target="tpu_custom_call" | custom-call | tf_op jit(solution)/shard_map/pallas_call | solution.py:437
  54.8 3.8 %copy.8 = f32[1280,640]{1,0:T(8,128)} copy(f32[1280,640]{1,0:T(8,128)} %shard_map.64) | data formatting | bytes 6553600
